TPU v7x, 128 devices: a whole 4x4x4 slice. The times are simulated.
128 devices in a mesh: tok: 8 (over x_lo, z), ffn: 16 (over y, x_hi, core).
Axes of the slice: x: 4 (x_hi: 2, x_lo: 2; x = x_hi * 2 + x_lo), y: 4, z: 4, core: 2. Of those that a mesh axis runs over, the one named last changes fastest.
Arguments:
- tokens: bfloat16 [2, 8192, 1024], P(None, ('tok', 'ffn')), may hold values from -6 to 6
- memory: bfloat16 [2, 4096, 1024], P(None, ('tok', 'ffn')), may hold values from -6 to 6
- segment_ids: int32 [2, 8192], P(None, 'tok'), may hold values from 0 to 2, as said below
- buckets: int32 [1024], replicated, may hold values from 0 to 31, as said below
- w_query: bfloat16 [1024, 1024], P(('tok', 'ffn')), may hold values from -0.1875 to 0.1875
- w_keyval: bfloat16 [1024, 1024], P(('tok', 'ffn')), may hold values from -0.1875 to 0.1875
- w_output: bfloat16 [1024, 1024], P(('tok', 'ffn')), may hold values from -1.5 to 1.5
- w_cross_query: bfloat16 [1024, 1024], P(('tok', 'ffn')), may hold values from -0.1875 to 0.1875
- w_cross_keyval: bfloat16 [1024, 1024], P(('tok', 'ffn')), may hold values from -0.1875 to 0.1875
- w_cross_output: bfloat16 [1024, 1024], P(('tok', 'ffn')), may hold values from -1.5 to 1.5
- norm_self: bfloat16 [1024], P(('tok', 'ffn')), may hold values from 0.5 to 1.5
- norm_cross: bfloat16 [1024], P(('tok', 'ffn')), may hold values from 0.5 to 1.5
- norm_ffn: bfloat16 [1024], P(('tok', 'ffn')), may hold values from 0.5 to 1.5
- bias_table: bfloat16 [512], P(('tok', 'ffn')), may hold values from -4 to 4
- w_gate: bfloat16 [1024, 2816], P('tok', 'ffn'), may hold values from -0.1875 to 0.1875
- w_up: bfloat16 [1024, 2816], P('tok', 'ffn'), may hold values from -0.1875 to 0.1875
- w_down: bfloat16 [2816, 1024], P('ffn', 'tok'), may hold values from -0.109375 to 0.109375
- cotangent: bfloat16 [2, 8192, 1024], P(None, ('tok', 'ffn')), may hold values from -6 to 6
Outputs:
- output: float32 [2, 8192, 1024], P(None, ('tok', 'ffn'))
- d_tokens: float32 [2, 8192, 1024], P(None, ('tok', 'ffn'))
- d_memory: float32 [2, 4096, 1024], P(None, ('tok', 'ffn'))
- d_w_query: float32 [1024, 1024], P(('tok', 'ffn'))
- d_w_keyval: float32 [1024, 1024], P(('tok', 'ffn'))
- d_w_output: float32 [1024, 1024], P(('tok', 'ffn'))
- d_w_cross_query: float32 [1024, 1024], P(('tok', 'ffn'))
- d_w_cross_keyval: float32 [1024, 1024], P(('tok', 'ffn'))
- d_w_cross_output: float32 [1024, 1024], P(('tok', 'ffn'))
- d_norm_self: float32 [1024], P(('tok', 'ffn'))
- d_norm_cross: float32 [1024], P(('tok', 'ffn'))
- d_norm_ffn: float32 [1024], P(('tok', 'ffn'))
- d_bias_table: float32 [512], P(('tok', 'ffn'))
- d_w_gate: float32 [1024, 2816], P('tok', 'ffn')
- d_w_up: float32 [1024, 2816], P('tok', 'ffn')
- d_w_down: float32 [2816, 1024], P('ffn', 'tok')
Inputs may be any that keep to these rules, and one draw needn't show every extreme that they name: `segment_ids`: within a sequence the ids never fall; document 1 starts within the first 64 positions and ends within the last 64, documents 0 and 2 fill the rest. buckets never fall as the distance grows, buckets[d] = d for d < 16, and the last entry is 31.
All inputs are finite; a program needn't handle non-finite values.
Results may differ from a plain program's by a relative error of at most 0.04.
Values may be sent and summed in bfloat16 or wider, within the bound.
No kernel may reach another device: no remote copies, remote signals or barrier semaphores. Data moves between devices by JAX's collectives and lax.ppermute only.
A program may use at most 384 MiB of HBM per device.

v0:
```python
import jax
import jax.numpy as jnp
from jax import lax
from jax.sharding import PartitionSpec as P

HEADS = 16
HEAD_DIM = 64
BUCKETS = 32
KV_HEADS = 8


epsilon = 1e-06
masked_score = -1e30


def gather_turned(arrays, axis, dims):
    turned = [jnp.moveaxis(a, dim, 0) for a, dim in zip(arrays, dims)]
    both = jnp.concatenate([t.reshape(len(t), -1) for t in turned], axis=1)
    whole, at, finished = (lax.all_gather(both, axis, axis=0, tiled=True), 0, [])
    for t, dim in zip(turned, dims):
        share = whole[:, at : at + t[0].size].reshape(-1, *t.shape[1:])
        finished.append(jnp.moveaxis(share, 0, dim))
        at += t[0].size
    return tuple(finished)


def laid_out(tiles, dim):
    tiles = jnp.moveaxis(tiles, 0, dim)
    dims = tiles.shape
    return tiles.reshape(*dims[:dim], dims[dim] * dims[dim + 1], *dims[dim + 2 :])


def gather_together(arrays, axis, dims):
    ravelled = jnp.concatenate([a.reshape(-1) for a in arrays])
    lines, at, finished = (lax.all_gather(ravelled, axis), 0, [])
    for a, dim in zip(arrays, dims):
        tiles = lines[:, at : at + a.size].reshape(-1, *a.shape)
        finished.append(laid_out(tiles, dim))
        at += a.size
    return tuple(finished)


def in_blocks(x, dim, devices):
    before, after = (x.shape[:dim], x.shape[dim + 1 :])
    return jnp.moveaxis(x.reshape(*before, devices, -1, *after), dim, 0)


def sum_together(arrays, axis, dims):
    devices = lax.axis_size(axis)
    tiles = [in_blocks(a, dim, devices) for a, dim in zip(arrays, dims)]
    lines = jnp.concatenate([b.reshape(devices, -1) for b in tiles], axis=1)
    extent = max(16, -(-lines.shape[1] // 1024) * 8)
    lines = jnp.pad(lines, ((0, 0), (0, extent * 128 - lines.shape[1]))).reshape(-1, 128)
    ravelled, at, finished = (lax.psum_scatter(lines, axis, tiled=True).reshape(-1), 0, [])
    for b in tiles:
        part = b[0]
        finished.append(ravelled[at : at + part.size].reshape(part.shape))
        at += part.size
    return tuple(finished)


def sent_together(arrays, axis, dim, along):
    widths = [a.shape[along] for a in arrays]
    both = jnp.concatenate(arrays, axis=along)
    whole = lax.psum_scatter(both, axis, scatter_dimension=dim, tiled=True)
    return tuple(jnp.split(whole, [sum(widths[:k]) for k in range(1, len(widths))], axis=along))


def scaled_norm(values, gains):
    inverse = lax.rsqrt(jnp.mean(values * values, axis=-1, keepdims=True) + epsilon)
    return values * inverse * gains


def product(left, right):
    return jnp.dot(left, right, preferred_element_type=jnp.float32)


def left_transposed(left, right):
    return lax.dot_general(
        left, right, (((0,), (0,)), ((), ())), preferred_element_type=jnp.float32
    )


def right_transposed(left, right):
    return lax.dot_general(
        left, right, (((1,), (1,)), ((), ())), preferred_element_type=jnp.float32
    )


def split_heads(keyvals):
    half_width = KV_HEADS * HEAD_DIM
    key_heads = keyvals[:, :half_width].reshape(-1, KV_HEADS, HEAD_DIM)
    value_heads = keyvals[:, half_width:].reshape(-1, KV_HEADS, HEAD_DIM)
    return (key_heads, value_heads)


def scores_of(query_heads, key_heads, bias_terms, allowed, scaling):
    raw_scores = jnp.einsum(
        "qngd,knd->ngqk", query_heads, key_heads, preferred_element_type=jnp.float32
    )
    return jnp.where(allowed, raw_scores * scaling + bias_terms, masked_score)


def attend(query_heads, key_heads, value_heads, bias_terms, allowed, scaling):
    scores = scores_of(query_heads, key_heads, bias_terms, allowed, scaling)
    highest = jnp.max(scores, axis=-1, keepdims=True)
    exponent = jnp.exp(scores - highest)
    totals = jnp.sum(exponent, axis=-1, keepdims=True)
    attention = (exponent / totals).astype(jnp.bfloat16)
    output = jnp.einsum(
        "ngqk,knd->qngd", attention, value_heads, preferred_element_type=jnp.float32
    )
    return (output, highest + jnp.log(totals))


def attend_back(
    query_heads, key_heads, value_heads, bias_terms, allowed, scaling, logsum, grad_output
):
    scores = scores_of(query_heads, key_heads, bias_terms, allowed, scaling)
    attention = jnp.exp(scores - logsum)
    grad_attention = jnp.einsum(
        "qngd,knd->ngqk", grad_output, value_heads, preferred_element_type=jnp.float32
    )
    centre = jnp.sum(grad_attention * attention, axis=-1, keepdims=True)
    grad_scores = (attention * (grad_attention - centre)).astype(jnp.bfloat16)
    grad_query = (
        jnp.einsum("ngqk,knd->qngd", grad_scores, key_heads, preferred_element_type=jnp.float32)
        * scaling
    )
    grad_keys = (
        jnp.einsum("ngqk,qngd->knd", grad_scores, query_heads, preferred_element_type=jnp.float32)
        * scaling
    )
    grad_values = jnp.einsum(
        "ngqk,qngd->knd",
        attention.astype(jnp.bfloat16),
        grad_output,
        preferred_element_type=jnp.float32,
    )
    return (grad_query, grad_keys, grad_values, grad_scores)


def add_up(total, extra):
    if total is None:
        return extra
    return jax.tree.map(jnp.add, total, extra)


def on_device(
    tokens,
    memory,
    segment_ids,
    buckets,
    w_query,
    w_keyval,
    w_output,
    w_cross_query,
    w_cross_keyval,
    w_cross_output,
    norm_self,
    norm_cross,
    norm_ffn,
    bias_table,
    w_gate,
    w_up,
    w_down,
    cotangent,
):
    local_row_count = tokens.shape[1]
    width = tokens.shape[2]
    length = segment_ids.shape[1]
    groups = HEADS // KV_HEADS
    scaling = HEAD_DIM ** (-0.5)
    ffn_local = gather_turned((w_gate, w_up, w_down), "tok", (0, 0, 1))
    ffn_used = gather_turned((ffn_local[0], ffn_local[1], ffn_local[2]), "ffn", (1, 1, 0))
    gate_up = jnp.concatenate([ffn_used[0], ffn_used[1]], axis=1)
    down_used = ffn_used[2]
    hidden_cols = ffn_used[0].shape[1]
    first_row = lax.axis_index("ffn") * local_row_count
    query_pos = first_row + jnp.arange(local_row_count, dtype=jnp.int32)
    key_pos = jnp.arange(length, dtype=jnp.int32)
    distance = jnp.clip(query_pos[:, None] - key_pos[None, :], 0, length - 1)
    bucket_row_indices = buckets[distance]
    indicator_matrix = (
        bucket_row_indices[None] == jnp.arange(BUCKETS, dtype=jnp.int32)[:, None, None]
    ).astype(jnp.bfloat16)
    causal = key_pos[None, :] <= query_pos[:, None]

    def micro_step(batch_index, whole):
        (
            query_w,
            keyval_w,
            output_w,
            cross_query_w,
            cross_keyval_w,
            cross_output_w,
            gain_self,
            gain_cross,
            feedforward_gain,
            table,
        ) = whole
        gain_self = gain_self.astype(jnp.float32)
        gain_cross = gain_cross.astype(jnp.float32)
        feedforward_gain = feedforward_gain.astype(jnp.float32)
        bias_table_heads = table.reshape(HEADS, BUCKETS)
        segment_row = segment_ids[batch_index]
        segment_here = lax.dynamic_slice_in_dim(segment_row, first_row, local_row_count, 0)
        allowed = causal & (segment_row[None, :] == segment_here[:, None])
        bias_terms = jnp.einsum(
            "fn,nox->fox", bias_table_heads, indicator_matrix, preferred_element_type=jnp.float32
        )
        bias_terms = bias_terms.reshape(KV_HEADS, groups, local_row_count, length)
        inputs = tokens[batch_index].astype(jnp.float32)
        normed_self = scaled_norm(inputs, gain_self).astype(jnp.bfloat16)
        queries = product(normed_self, query_w).astype(jnp.bfloat16)
        keyvals = product(normed_self, keyval_w).astype(jnp.bfloat16)
        memory_rows = memory[batch_index]
        cross_keyvals = product(memory_rows, cross_keyval_w).astype(jnp.bfloat16)
        keyvals_all, cross_all = gather_together((keyvals, cross_keyvals), "ffn", (0, 0))
        key_self, value_self = split_heads(keyvals_all)
        query_heads = queries.reshape(local_row_count, KV_HEADS, groups, HEAD_DIM)
        attended, logsum_self = attend(
            query_heads, key_self, value_self, bias_terms, allowed, scaling
        )
        attended = attended.reshape(local_row_count, width).astype(jnp.bfloat16)
        after_self = inputs + product(attended, output_w)
        normed_cross = scaled_norm(after_self, gain_cross).astype(jnp.bfloat16)
        cross_queries = product(normed_cross, cross_query_w).astype(jnp.bfloat16)
        key_cross, value_cross = split_heads(cross_all)
        cross_heads = cross_queries.reshape(local_row_count, KV_HEADS, groups, HEAD_DIM)
        crossed, logsum_cross = attend(cross_heads, key_cross, value_cross, 0.0, True, scaling)
        crossed = crossed.reshape(local_row_count, width).astype(jnp.bfloat16)
        after_cross = after_self + product(crossed, cross_output_w)
        normed_ffn = scaled_norm(after_cross, feedforward_gain).astype(jnp.bfloat16)
        pre_active = product(normed_ffn, gate_up)
        activated, active_pull = jax.vjp(
            lambda gate_in, up_in: jax.nn.gelu(gate_in, approximate=True) * up_in,
            pre_active[:, :hidden_cols],
            pre_active[:, hidden_cols:],
        )
        hidden = activated.astype(jnp.bfloat16)
        ffn_result = product(hidden, down_used)
        result = after_cross + ffn_result
        grad_result = cotangent[batch_index]
        grad_hidden = right_transposed(grad_result, down_used)
        grad_down = left_transposed(hidden, grad_result)
        grad_gate, grad_upper = active_pull(grad_hidden)
        grad_pre = jnp.concatenate([grad_gate, grad_upper], axis=1).astype(jnp.bfloat16)
        grad_gate_up = left_transposed(normed_ffn, grad_pre)
        grad_normed_ffn = right_transposed(grad_pre, gate_up)
        _, ffn_pull = jax.vjp(scaled_norm, after_cross, feedforward_gain)
        grad_from_ffn, grad_gain_ffn = ffn_pull(grad_normed_ffn)
        grad_after_cross = grad_result.astype(jnp.float32) + grad_from_ffn
        grad_cross_branch = grad_after_cross.astype(jnp.bfloat16)
        grad_crossed = right_transposed(grad_cross_branch, cross_output_w).astype(jnp.bfloat16)
        grad_cross_output = left_transposed(crossed, grad_cross_branch)
        grad_cq, grad_ck, grad_cv, _ = attend_back(
            cross_heads,
            key_cross,
            value_cross,
            0.0,
            True,
            scaling,
            logsum_cross,
            grad_crossed.reshape(local_row_count, KV_HEADS, groups, HEAD_DIM),
        )
        grad_cross_queries = grad_cq.reshape(local_row_count, width).astype(jnp.bfloat16)
        grad_cross_part = jnp.concatenate(
            [grad_ck.reshape(grad_ck.shape[0], -1), grad_cv.reshape(grad_cv.shape[0], -1)], axis=1
        )
        grad_cross_query = left_transposed(normed_cross, grad_cross_queries)
        _, cross_pull = jax.vjp(scaled_norm, after_self, gain_cross)
        grad_from_cross, grad_gain_cross = cross_pull(
            right_transposed(grad_cross_queries, cross_query_w)
        )
        grad_after_self = grad_after_cross + grad_from_cross
        grad_self_branch = grad_after_self.astype(jnp.bfloat16)
        grad_attended = right_transposed(grad_self_branch, output_w).astype(jnp.bfloat16)
        grad_output_w = left_transposed(attended, grad_self_branch)
        grad_sq, grad_sk, grad_sv, grad_scores = attend_back(
            query_heads,
            key_self,
            value_self,
            bias_terms,
            allowed,
            scaling,
            logsum_self,
            grad_attended.reshape(local_row_count, KV_HEADS, groups, HEAD_DIM),
        )
        grad_table = jnp.einsum(
            "xct,jct->xj",
            grad_scores.reshape(HEADS, local_row_count, length),
            indicator_matrix,
            preferred_element_type=jnp.float32,
        ).reshape(-1)
        grad_queries = grad_sq.reshape(local_row_count, width).astype(jnp.bfloat16)
        grad_self_part = jnp.concatenate(
            [grad_sk.reshape(grad_sk.shape[0], -1), grad_sv.reshape(grad_sv.shape[0], -1)], axis=1
        )
        grad_kv_here, grad_cross_here = sum_together(
            (grad_self_part, grad_cross_part), "ffn", (0, 0)
        )
        grad_keyvals = grad_kv_here.astype(jnp.bfloat16)
        cross_key_value_gradient = grad_cross_here.astype(jnp.bfloat16)
        grad_memory = right_transposed(cross_key_value_gradient, cross_keyval_w)
        grad_cross_keyval = left_transposed(memory_rows, cross_key_value_gradient)
        grad_query_w = left_transposed(normed_self, grad_queries)
        grad_keyval_w = left_transposed(normed_self, grad_keyvals)
        grad_normed_self = right_transposed(grad_queries, query_w) + right_transposed(
            grad_keyvals, keyval_w
        )
        _, self_pull = jax.vjp(scaled_norm, inputs, gain_self)
        grad_from_self, grad_gain_self = self_pull(grad_normed_self)
        grad_tokens = grad_after_self + grad_from_self
        attention_grads = (
            grad_query_w,
            grad_keyval_w,
            grad_output_w,
            grad_cross_query,
            grad_cross_keyval,
            grad_cross_output,
            grad_gain_self,
            grad_gain_cross,
            grad_gain_ffn,
            grad_table,
        )
        ffn_grads = (grad_gate_up[:, :hidden_cols], grad_gate_up[:, hidden_cols:], grad_down)
        return (result, grad_tokens, grad_memory, attention_grads, ffn_grads)

    results = []
    grad_inputs = []
    grad_memories = []
    ffn_total = None
    attention_portions = None
    micro_count = tokens.shape[0]
    for batch_index in range(micro_count):
        whole = gather_together(
            (
                w_query,
                w_keyval,
                w_output,
                w_cross_query,
                w_cross_keyval,
                w_cross_output,
                norm_self,
                norm_cross,
                norm_ffn,
                bias_table,
            ),
            ("tok", "ffn"),
            (0, 0, 0, 0, 0, 0, 0, 0, 0, 0),
        )
        outcome = micro_step(batch_index, whole)
        results.append(outcome[0])
        grad_inputs.append(outcome[1])
        grad_memories.append(outcome[2])
        ffn_total = add_up(ffn_total, outcome[4])
        (
            part_query,
            part_keyval,
            part_output,
            part_cross_query,
            part_cross_keyval,
            part_cross_output,
            part_gain_self,
            part_gain_cross,
            part_gain_ffn,
            part_table,
        ) = outcome[3]
        pieces = sum_together(
            (
                part_query,
                part_keyval,
                part_output,
                part_cross_query,
                part_cross_keyval,
                part_cross_output,
                part_gain_self,
                part_gain_cross,
                part_gain_ffn,
                part_table,
            ),
            ("tok", "ffn"),
            (0, 0, 0, 0, 0, 0, 0, 0, 0, 0),
        )
        attention_portions = add_up(attention_portions, pieces)
    ffn_group = (
        *sent_together((ffn_total[0], ffn_total[1]), "ffn", 1, 0),
        lax.psum_scatter(ffn_total[2], "ffn", scatter_dimension=0, tiled=True),
    )
    ffn_final = (
        *sent_together((ffn_group[0], ffn_group[1]), "tok", 0, 1),
        lax.psum_scatter(ffn_group[2], "tok", scatter_dimension=1, tiled=True),
    )
    return (
        jnp.stack(results),
        jnp.stack(grad_inputs),
        jnp.stack(grad_memories),
        attention_portions[0],
        attention_portions[1],
        attention_portions[2],
        attention_portions[3],
        attention_portions[4],
        attention_portions[5],
        attention_portions[6],
        attention_portions[7],
        attention_portions[8],
        attention_portions[9],
        ffn_final[0],
        ffn_final[1],
        ffn_final[2],
    )


def solution(mesh):
    placed = (
        P(None, ("tok", "ffn"), None),
        P(None, ("tok", "ffn"), None),
        P(None, "tok"),
        P(),
        P(("tok", "ffn"), None),
        P(("tok", "ffn"), None),
        P(("tok", "ffn"), None),
        P(("tok", "ffn"), None),
        P(("tok", "ffn"), None),
        P(("tok", "ffn"), None),
        P(("tok", "ffn")),
        P(("tok", "ffn")),
        P(("tok", "ffn")),
        P(("tok", "ffn")),
        P("tok", "ffn"),
        P("tok", "ffn"),
        P("ffn", "tok"),
        P(None, ("tok", "ffn"), None),
    )
    return jax.shard_map(
        on_device,
        mesh=mesh,
        in_specs=placed,
        out_specs=(
            P(None, ("tok", "ffn"), None),
            P(None, ("tok", "ffn"), None),
            P(None, ("tok", "ffn"), None),
            P(("tok", "ffn"), None),
            P(("tok", "ffn"), None),
            P(("tok", "ffn"), None),
            P(("tok", "ffn"), None),
            P(("tok", "ffn"), None),
            P(("tok", "ffn"), None),
            P(("tok", "ffn")),
            P(("tok", "ffn")),
            P(("tok", "ffn")),
            P(("tok", "ffn")),
            P("tok", "ffn"),
            P("tok", "ffn"),
            P("ffn", "tok"),
        ),
        check_vma=False,
    )
```

profile of v0, /device:TPU:1, one launch (start us, length us, event | category | flops | bytes accessed | tf_op | source)
XLA Modules:
  0.0 1570.1 jit_solution(16018953333727594996)
XLA Ops:
  22.5 175.2 %all-reduce.9.cloned.1.call-done = bf16[6295040]{0:T(1024)(128)(2,1)} async-done(((bf16[6295040]{0:T(1024)(128)(2,1)}), bf16[6295040]{0:T(1024)(128)(2,1)}) %all-reduce.9.cloned.1.call-update) | async-done | bytes 12590096
  197.7 31.0 %reshape.695 = bf16[128,49180]{1,0:T(8,128)(2,1)} reshape(bf16[6295040]{0:T(1024)(128)(2,1)} %all-reduce.9.cloned.1.call-done) | data formatting | bytes 25180160 | tf_op jit(solution)/shard_map/all_gather | solution.py:35
  228.7 9.2 fusion.207
  256.1 260.7 %gather_fusion = s32[65536]{0:T(1024)S(1)} fusion(s32[1024]{0:T(1024)S(1)} %copy-done, s32[65536]{0:T(1024)S(1)} %broadcast_clamp_fusion), kind=kCustom, calls=%fused_computation | custom fusion | bytes 786432 | tf_op jit(solution)/shard_map/gather | solution.py:183
  572.5 5.8 fusion.215
  585.6 5.5 fusion.216
  607.4 10.1 slice_bitcast_fusion.1
  617.6 6.6 fusion.192
  624.2 7.1 fusion.194
  631.3 5.5 fusion.109
  644.2 5.2 multiply_reduce_fusion.2
  730.3 5.9 pad_maximum_fusion.3
  751.9 5.2 pad_maximum_fusion.4
  761.4 6.2 pad_maximum_fusion.2
  773.3 12.2 fusion.110
  785.5 9.7 fusion.112
  795.2 24.3 %slice_add_fusion.1 = (f32[1024,2816]{1,0:T(8,128)}, f32[1024,2816]{1,0:T(8,128)}) fusion(f32[1024,5632]{1,0:T(8,128)} %fusion.110, f32[1024,5632]{1,0:T(8,128)} %fusion.112), kind=kLoop, calls=%fused_computation.3 | loop fusion | flops 5767168 | bytes 69206016 | tf_op jit(solution)/shard_map/add | solution.py:146
  819.5 17.7 %pad_maximum_fusion = f32[2048,2816]{1,0:T(8,128)} fusion(f32[1024,2816]{1,0:T(8,128)} %get-tuple-element.89, f32[1024,2816]{1,0:T(8,128)} %get-tuple-element.88), kind=kLoop, calls=%fused_computation.1 | loop fusion | flops 5767168 | bytes 46137344 | tf_op jit(solution)/shard_map/concatenate | solution.py:64
  837.2 24.1 %copy.157 = f32[2048,2816]{0,1:T(8,128)} copy(f32[2048,2816]{1,0:T(8,128)} %pad_maximum_fusion) | data formatting | bytes 46137344
  872.9 5.9 convolution_add_fusion
  888.5 5.2 reshape_reshape.116
  935.9 5.5 reshape_reshape.106
  946.6 6.5 reshape_reshape.113
  978.7 5.4 reshape_reshape.107
  986.8 5.4 copy.132
  1000.0 5.5 copy.134
  1035.3 17.3 %pad.8 = f32[128,50176]{1,0:T(8,128)} pad(f32[128,49180]{1,0:T(8,128)} %dynamic-update-slice.10, f32[]{:T(128)} %constant.18.clone.1), padding=0_0x0_996 | pad | bytes 50870276 | tf_op jit(solution)/shard_map/jit(_pad)/pad | solution.py:53
  1052.6 23.7 %reshape.679 = f32[50176,128]{1,0:T(8,128)} reshape(f32[128,50176]{1,0:T(8,128)} %pad.8) | data formatting | bytes 51380224 | tf_op jit(solution)/shard_map/reshape | solution.py:53
  1101.1 17.6 %pad.7 = f32[128,50176]{1,0:T(8,128)} pad(f32[128,49180]{1,0:T(8,128)} %dynamic-update-slice.20, f32[]{:T(128)} %constant.18.clone.1), padding=0_0x0_996 | pad | bytes 50870276 | tf_op jit(solution)/shard_map/jit(_pad)/pad | solution.py:53
  1118.7 24.6 %reshape.674 = f32[50176,128]{1,0:T(8,128)} reshape(f32[128,50176]{1,0:T(8,128)} %pad.7) | data formatting | bytes 51380224 | tf_op jit(solution)/shard_map/reshape | solution.py:53
  1160.3 69.1 %reduce-scatter.15.cloned.1.call-done = f32[176,1024]{1,0:T(8,128)} async-done(((f32[2816,1024]{1,0:T(8,128)}), f32[176,1024]{1,0:T(8,128)}) %reduce-scatter.15.cloned.1.call-update) | async-done | bytes 720912 | tf_op jit(solution)/shard_map/reduce_scatter | solution.py:389
  1229.5 322.6 %all-reduce.11.cloned.1.call-done = (f32[50176,128]{1,0:T(8,128)}, f32[50176,128]{1,0:T(8,128)}) async-done(((f32[50176,128]{1,0:T(8,128)}, f32[50176,128]{1,0:T(8,128)}), (f32[50176,128]{1,0:T(8,128)}, f32[50176,128]{1,0:T(8,128)})) %all-reduce.11.cloned.1.call-update) | async-done | bytes 51380240
  (618 shorter events, 410.6 us)
Async XLA Ops:
  8.0 248.0 %copy-start = (s32[1024]{0:T(1024)S(1)}, s32[1024]{0:T(1024)}, u32[]{:S(2)}) copy-start(s32[1024]{0:T(1024)} %param.21) | copy-start | bytes 12292
  8.0 189.7 %all-reduce.9.cloned.1.call-start = ((), (), s32[]{:S(2)}) async-start(), calls=%async_computation.15 | async-start | bytes 25182208
  20.8 232.4 %all-gather.8.cloned.1.call-start = ((), (), s32[]{:S(2)}) async-start(), calls=%async_computation.6 | async-start | bytes 1216512 | tf_op jit(solution)/shard_map/all_gather | solution.py:19
  22.3 515.9 %all-gather.12.cloned.1.call-start = ((), (), s32[]{:S(2)}) async-start(), calls=%async_computation.13 | async-start | bytes 3342336 | tf_op jit(solution)/shard_map/all_gather | solution.py:35
  22.5 206.2 %copy-start.154 = (f32[64]{0:T(128)}, f32[64]{0:T(128)S(1)}, u32[]{:S(2)}) copy-start(f32[64]{0:T(128)S(1)} %get-tuple-element.79) | copy-start | bytes 772
  22.5 206.2 %copy-start.156 = (f32[64]{0:T(128)}, f32[64]{0:T(128)S(1)}, u32[]{:S(2)}) copy-start(f32[64]{0:T(128)S(1)} %get-tuple-element.78) | copy-start | bytes 772
  22.5 509.5 %copy-start.137 = (f32[64]{0:T(128)}, f32[64]{0:T(128)S(1)}, u32[]{:S(2)}) copy-start(f32[64]{0:T(128)S(1)} %get-tuple-element.173) | copy-start | bytes 772
  22.5 510.9 %copy-start.135 = (f32[64]{0:T(128)}, f32[64]{0:T(128)S(1)}, u32[]{:S(2)}) copy-start(f32[64]{0:T(128)S(1)} %get-tuple-element.172) | copy-start | bytes 772
  239.0 294.5 %copy-start.103 = (f32[1024]{0:T(1024)}, f32[1024]{0:T(1024)S(1)}, u32[]{:S(2)}) copy-start(f32[1024]{0:T(1024)S(1)} %reshape.683) | copy-start | bytes 12292
  249.7 292.4 %all-gather.14.cloned.1.call-start = ((), (), s32[]{:S(2)}) async-start(), calls=%async_computation.14 | async-start | bytes 3342336 | tf_op jit(solution)/shard_map/all_gather | solution.py:35
  253.1 354.3 %all-gather.10.cloned.1.call-start = ((), (), s32[]{:S(2)}) async-start(), calls=%async_computation.7 | async-start | bytes 18382848 | tf_op jit(solution)/shard_map/all_gather | solution.py:19
  255.6 707.2 %reduce-scatter.11.cloned.1.call-start = ((), (), s32[]{:S(2)}) async-start(), calls=%async_computation.9 | async-start | bytes 6684672 | tf_op jit(solution)/shard_map/reduce_scatter | solution.py:54
  256.1 260.8 %copy-start.145 = (s32[2,1024]{1,0:T(2,128)S(1)}, s32[2,1024]{1,0:T(2,128)}, u32[]{:S(2)}) copy-start(s32[2,1024]{1,0:T(2,128)} %param.20) | copy-start | bytes 24580
  516.8 18.0 %copy-start.96 = (s32[64,1024]{1,0:T(8,128)}, s32[64,1024]{1,0:T(8,128)S(1)}, u32[]{:S(2)}) copy-start(s32[64,1024]{1,0:T(8,128)S(1)} %reshape.688) | copy-start | bytes 786436
  603.1 41.1 %copy-start.65 = (f32[64,1024]{1,0:T(8,128)}, f32[64,1024]{1,0:T(8,128)S(1)}, u32[]{:S(2)}) copy-start(f32[64,1024]{1,0:T(8,128)S(1)} %get-tuple-element.154) | copy-start | bytes 786436
  603.1 46.3 %copy-start.141 = (f32[64]{0:T(128)}, f32[64]{0:T(128)S(1)}, u32[]{:S(2)}) copy-start(f32[64]{0:T(128)S(1)} %fusion.179) | copy-start | bytes 772
  605.5 43.9 %copy-start.143 = (f32[64]{0:T(128)}, f32[64]{0:T(128)S(1)}, u32[]{:S(2)}) copy-start(f32[64]{0:T(128)S(1)} %fusion.182) | copy-start | bytes 772
  631.3 10.0 slice-start.4
  650.6 22.7 %copy-start.55 = (f32[64,1024]{1,0:T(8,128)}, f32[64,1024]{1,0:T(8,128)S(1)}, u32[]{:S(2)}) copy-start(f32[64,1024]{1,0:T(8,128)S(1)} %get-tuple-element.125) | copy-start | bytes 786436
  673.5 225.2 %copy-start.53 = (f32[64,1024]{1,0:T(8,128)}, f32[64,1024]{1,0:T(8,128)S(1)}, u32[]{:S(2)}) copy-start(f32[64,1024]{1,0:T(8,128)S(1)} %get-tuple-element.132) | copy-start | bytes 786436
  673.5 232.9 %copy-start.51 = (f32[64,1024]{1,0:T(8,128)}, f32[64,1024]{1,0:T(8,128)S(1)}, u32[]{:S(2)}) copy-start(f32[64,1024]{1,0:T(8,128)S(1)} %get-tuple-element.131) | copy-start | bytes 786436
  741.2 222.5 %reduce-scatter.9.cloned.1.call-start = ((), (), s32[]{:S(2)}) async-start(), calls=%async_computation.8 | async-start | bytes 6684672 | tf_op jit(solution)/shard_map/reduce_scatter | solution.py:54
  772.7 12.8 copy-start.66
  772.7 12.8 copy-start.142
  772.7 370.7 %reduce-scatter.19.cloned.1.call-start = ((), (), s32[]{:S(2)}) async-start(), calls=%async_computation.16 | async-start | bytes 24510464
  773.3 12.2 copy-start.110
  773.3 12.2 copy-start.112
  861.4 368.1 %reduce-scatter.15.cloned.1.call-start = ((), (), s32[]{:S(2)}) async-start(), calls=%async_computation.11 | async-start | bytes 12255232 | tf_op jit(solution)/shard_map/reduce_scatter | solution.py:389
  878.9 673.2 %all-reduce.11.cloned.1.call-start = ((), (), s32[]{:S(2)}) async-start(), calls=%async_computation.17 | async-start | bytes 102760448
  1143.3 416.6 %reduce-scatter.13.cloned.1.call-start = ((), (), s32[]{:S(2)}) async-start(), calls=%async_computation.10 | async-start | bytes 1769472 | tf_op jit(solution)/shard_map/reduce_scatter | solution.py:65
  1147.1 415.4 %reduce-scatter.17.cloned.1.call-start = ((), (), s32[]{:S(2)}) async-start(), calls=%async_computation.12 | async-start | bytes 811008 | tf_op jit(solution)/shard_map/reduce_scatter | solution.py:393
  1157.0 405.5 %copy-start.1 = (s32[1024]{0:T(1024)S(1)}, s32[1024]{0:T(1024)}, u32[]{:S(2)}) copy-start(s32[1024]{0:T(1024)} %param.21) | copy-start | bytes 12292
  (153 other events, 640.6 us)
Sparse Core Ops, SparseCore 0:
  20.9 176.7 all-reduce.8
  1143.5 408.5 all-reduce.10
Sparse Core Ops, SparseCore 1:
  23.4 39.7 all-gather.7
  249.8 49.3 all-gather.11
  302.1 49.5 all-gather.13
  354.1 110.0 all-gather.9
  741.3 86.3 reduce-scatter.10
  832.5 88.3 reduce-scatter.8
  925.8 177.2 reduce-scatter.18
  1107.8 121.6 reduce-scatter.14
  1231.7 39.2 reduce-scatter.12
  1273.9 41.1 reduce-scatter.16
where the time goes:
time: 1580 us; the launch traced here: 1570 us
  local copies, waits for them, and re-layouts  692 us (44%)
  waiting for transfers between devices  567 us (36%)
  matrix products  194 us (12%)
  other arithmetic  98 us (6%)
  between operations  17.9 us (1%)
    unnamed x15, waiting for transfers between devices  498 us
    gather x2, local copies, waits for them, and re-layouts, on_device(): bucket_row_indices = buckets[distance]  261 us
    unnamed x368, local copies, waits for them, and re-layouts  99.4 us
    another operation x16, local copies, waits for them, and re-layouts, sum_together(): lines = jnp.concatenate([b.reshape(devices, -1) for b in tiles], axis=1)  75.3 us
    reduce_scatter x1, waiting for transfers between devices, on_device(): lax.psum_scatter(ffn_total[2], 'ffn', scatter_dimension=0, tiled=True)  69.1 us
    dot_general x16, matrix products, left_transposed(): lax.dot_general(left, right, (((0,), (0,)), ((), ())), preferred_element_...  63.3 us
    reshape x4, local copies, waits for them, and re-layouts, sum_together(): jnp.pad(lines, ((0, 0), (0, extent * 128 - lines.shape[1])))  58.3 us
    all_gather x3, local copies, waits for them, and re-layouts, gather_together(): lines, at, finished = (lax.all_gather(ravelled, axis), 0, [])  38.7 us
  transfers between devices with their start and end apart: 12, of which 3 were waited for; matrix products, arithmetic and copies ran while one was open for 52% of the time, Pallas kernels for 0%

commit v1 on v0

v1 whole, which is shorter than its diff:
```python
import jax
import jax.numpy as jnp
from jax import lax
from jax.experimental import pallas as pl
from jax.experimental.pallas import tpu as pltpu
from jax.sharding import Mesh, PartitionSpec as P

HEADS = 16
HEAD_DIM = 64
BUCKETS = 32
KV_HEADS = 8
D = 1024
HALF = 512
SEQ = 1024
MEM = 512
BLOCK = 256

epsilon = 1e-06
masked_score = -1e30
scaling = HEAD_DIM ** (-0.5)

bf16 = jnp.bfloat16
f32 = jnp.float32

FFN = ("y", "xh", "c")
CHIPS = ("xl", "z", "y", "xh")
EVERY = ("xl", "z", "y", "xh", "c")


def dot(a, b):
    return lax.dot_general(a, b, (((1,), (0,)), ((), ())), preferred_element_type=f32)


def dot_nt(a, b):
    return lax.dot_general(a, b, (((1,), (1,)), ((), ())), preferred_element_type=f32)


def dot_tn(a, b):
    return lax.dot_general(a, b, (((0,), (0,)), ((), ())), preferred_element_type=f32)


def inverse_rms(a):
    return lax.rsqrt(jnp.mean(a * a, axis=-1, keepdims=True) + epsilon)


def norm_back(a, gain, e):
    n = inverse_rms(a)
    weighted = e * gain
    centre = jnp.mean(weighted * a, axis=-1, keepdims=True)
    grad_a = n * weighted - a * (n * n * n * centre)
    grad_gain = jnp.sum(e * a * n, axis=0, keepdims=True)
    return grad_a, grad_gain


def call(kernel, outs, *args, scratch=(), limit=48):
    return pl.pallas_call(
        kernel,
        out_shape=tuple(jax.ShapeDtypeStruct(s, t) for s, t in outs),
        scratch_shapes=list(scratch),
        compiler_params=pltpu.CompilerParams(vmem_limit_bytes=limit * 1024 * 1024),
    )(*args)


def to_all(x, axes):
    n = lax.axis_size(axes)
    return lax.all_to_all(jnp.broadcast_to(x[None], (n, *x.shape)), axes, 0, 0, tiled=True)


def exchange(x, axes):
    return lax.all_to_all(x, axes, 0, 0, tiled=True)


def sum_of_all(x, axes):
    return jnp.sum(exchange(x, axes).astype(f32), axis=0)


def swap_core(x):
    return lax.ppermute(x, "c", [(0, 1), (1, 0)])


def project_kernel(tok_ref, gain_ref, wq_ref, wkv_ref, out_ref, normed_ref):
    x = tok_ref[...].reshape(128, D).astype(f32)
    normed = (x * inverse_rms(x) * gain_ref[...]).astype(bf16)
    normed_ref[...] = normed
    for half in range(2):
        q = (dot(normed, wq_ref[half]) * scaling).astype(bf16)
        for k in range(8):
            one = q[:, k * 64 : (k + 1) * 64]
            out_ref[half * 8 + k, 0:64, :] = jnp.concatenate([one[0:64], one[64:128]], axis=1)
    keys = dot(normed, wkv_ref[0]).astype(bf16)
    values = dot(normed, wkv_ref[1]).astype(bf16)
    for n in range(KV_HEADS):
        both = jnp.concatenate(
            [keys[:, n * 64 : (n + 1) * 64], values[:, n * 64 : (n + 1) * 64]], axis=1
        )
        out_ref[2 * n, 64:192, :] = both
        out_ref[2 * n + 1, 64:192, :] = both


def bias_rows(onehot, table):
    return jnp.sum(onehot * table, axis=0, keepdims=True)


def self_kernel(qkv_ref, table_ref, turned_ref, seg_row_ref, seg_col_ref, out_ref, o_ref, p_ref):
    numbers = lax.broadcasted_iota(jnp.int32, (BUCKETS, SEQ), 0)
    onehot = (numbers == turned_ref[...]).astype(f32)
    terms = bias_rows(onehot, table_ref[...])
    bias = pltpu.roll(
        jnp.broadcast_to(terms, (BLOCK, SEQ)), 0, 1, stride=1, stride_axis=0
    )
    row = lax.broadcasted_iota(jnp.int32, (BLOCK, BLOCK), 0)
    col = lax.broadcasted_iota(jnp.int32, (BLOCK, BLOCK), 1)
    blocks = [jnp.where(col <= row, bias[:, 0:BLOCK], masked_score)]
    for k in range(1, 4):
        blocks.append(bias[:, SEQ - k * BLOCK : SEQ - (k - 1) * BLOCK])
    for mb in range(2):
        kv = qkv_ref[:, 64 + 64 * mb : 128 + 64 * mb, :].reshape(SEQ, 128)
        keys, values = kv[:, 0:64], kv[:, 64:128]
        for i in range(4):
            length = (i + 1) * BLOCK
            q = qkv_ref[4 * i : 4 * i + 4, 0:64, :].reshape(BLOCK, 128)
            q = q[:, mb * 64 : (mb + 1) * 64]
            s = dot_nt(q, keys[0:length])
            terms_here = jnp.concatenate([blocks[i - j] for j in range(i + 1)], axis=1)
            seg_q = seg_col_ref[mb, i * BLOCK : (i + 1) * BLOCK, :]
            seg_k = seg_row_ref[mb : mb + 1, 0:length]
            s = jnp.where(seg_q == seg_k, s + terms_here, masked_score)
            top = jnp.max(s, axis=-1, keepdims=True)
            e = jnp.exp(s - top)
            total = jnp.sum(e, axis=-1, keepdims=True)
            p = (e * (1.0 / total)).astype(bf16)
            p_ref[mb, i * BLOCK : (i + 1) * BLOCK, 0:length] = p
            o = dot(p, values[0:length])
            o_ref[i * BLOCK : (i + 1) * BLOCK, mb * 64 : (mb + 1) * 64] = o
            out_ref[4 * i : 4 * i + 4, :, mb * 64 : (mb + 1) * 64] = o.astype(bf16).reshape(
                4, 64, 64
            )


def self_back_kernel(qkv_ref, go_ref, o_ref, p_ref, turned_ref, out_ref, table_ref, diag_ref):
    diag_ref[...] = jnp.zeros_like(diag_ref)
    for mb in range(2):
        lanes = slice(mb * 64, (mb + 1) * 64)
        kv = qkv_ref[:, 64 + 64 * mb : 128 + 64 * mb, :].reshape(SEQ, 128)
        keys, values = kv[:, 0:64], kv[:, 64:128]
        grad_keys = [jnp.zeros((BLOCK, 64), f32) for _ in range(4)]
        grad_values = [jnp.zeros((BLOCK, 64), f32) for _ in range(4)]
        for i in range(4):
            length = (i + 1) * BLOCK
            q = qkv_ref[4 * i : 4 * i + 4, 0:64, :].reshape(BLOCK, 128)[:, lanes]
            go = go_ref[4 * i : 4 * i + 4, :, :].reshape(BLOCK, 128)[:, lanes]
            o = o_ref[i * BLOCK : (i + 1) * BLOCK, lanes]
            centre = jnp.sum(go.astype(f32) * o, axis=-1, keepdims=True)
            p = p_ref[mb, i * BLOCK : (i + 1) * BLOCK, 0:length]
            ds = p.astype(f32) * (dot_nt(go, values[0:length]) - centre)
            for j in range(i + 1):
                diag_ref[i - j] += ds[:, j * BLOCK : (j + 1) * BLOCK]
            ds = ds.astype(bf16)
            gq = (dot(ds, keys[0:length]) * scaling).astype(bf16)
            out_ref[4 * i : 4 * i + 4, 0:64, lanes] = gq.reshape(4, 64, 64)
            for j in range(i + 1):
                part = slice(j * BLOCK, (j + 1) * BLOCK)
                grad_keys[j] += dot_tn(ds[:, part], q)
                grad_values[j] += dot_tn(p[:, part], go)
        for j in range(4):
            both = jnp.concatenate([grad_keys[j], grad_values[j]], axis=1).astype(bf16)
            out_ref[4 * j : 4 * j + 4, 64 + 64 * mb : 128 + 64 * mb, :] = both.reshape(4, 64, 128)
    total = jnp.zeros((8, SEQ), f32)
    for g in range(BLOCK // 8):
        rows = slice(8 * g, 8 * g + 8)
        line = jnp.concatenate(
            [diag_ref[0, rows], diag_ref[3, rows], diag_ref[2, rows], diag_ref[1, rows]], axis=1
        )
        total = total + pltpu.roll(line, (SEQ - 8 * g) % SEQ, 1)
    sums = total[0:1]
    for s in range(1, 8):
        sums = sums + pltpu.roll(total[s : s + 1], SEQ - s, 1)
    numbers = lax.broadcasted_iota(jnp.int32, (BUCKETS, SEQ), 0)
    onehot = (numbers == turned_ref[...]).astype(f32)
    table_ref[...] = jnp.sum(onehot * sums, axis=1, keepdims=True)


def memory_kernel(mem_ref, w_ref, out_ref):
    for mb in range(2):
        rows = mem_ref[:, :, mb].reshape(MEM, D)
        keys = dot(rows, w_ref[0]).astype(bf16)
        values = dot(rows, w_ref[1]).astype(bf16)
        for n in range(KV_HEADS):
            part = slice(n * 64, (n + 1) * 64)
            out_ref[mb, n] = jnp.concatenate([keys[:, part], values[:, part]], axis=1)


def middle_kernel(
    att_ref, tok_ref, gain_cross_ref, gain_ffn_ref, wo_ref, wcq_ref, wco_ref, kv_ref,
    attended_ref, after_self_ref, normed_cross_ref, queries_ref, p_ref, crossed_ref,
    after_cross_ref, normed_ffn_ref,
):
    for h in range(HEADS):
        for mb in range(2):
            attended_ref[mb * 64 : (mb + 1) * 64, h * 64 : (h + 1) * 64] = att_ref[
                h, :, mb * 64 : (mb + 1) * 64
            ]
    attended = attended_ref[...]
    x = tok_ref[...].reshape(128, D).astype(f32)
    branch = jnp.concatenate([dot(attended, wo_ref[0]), dot(attended, wo_ref[1])], axis=1)
    after_self = x + branch
    after_self_ref[...] = after_self
    normed = (after_self * inverse_rms(after_self) * gain_cross_ref[...]).astype(bf16)
    normed_cross_ref[...] = normed
    for half in range(2):
        q = (dot(normed, wcq_ref[half]) * scaling).astype(bf16)
        queries_ref[:, half * HALF : (half + 1) * HALF] = q
    for mb in range(2):
        rows = slice(mb * 64, (mb + 1) * 64)
        for n in range(KV_HEADS):
            first = slice(2 * n * 64, (2 * n + 1) * 64)
            second = slice((2 * n + 1) * 64, (2 * n + 2) * 64)
            q = jnp.concatenate([queries_ref[rows, first], queries_ref[rows, second]], axis=0)
            kv = kv_ref[mb, n]
            s = dot_nt(q, kv[:, 0:64])
            e = jnp.exp(s - jnp.max(s, axis=-1, keepdims=True))
            p = (e * (1.0 / jnp.sum(e, axis=-1, keepdims=True))).astype(bf16)
            p_ref[mb, n] = p
            o = dot(p, kv[:, 64:128]).astype(bf16)
            crossed_ref[rows, first] = o[0:64]
            crossed_ref[rows, second] = o[64:128]
    crossed = crossed_ref[...]
    branch = jnp.concatenate([dot(crossed, wco_ref[0]), dot(crossed, wco_ref[1])], axis=1)
    after_cross = after_self + branch
    after_cross_ref[...] = after_cross
    normed_ffn_ref[...] = (
        after_cross * inverse_rms(after_cross) * gain_ffn_ref[...]
    ).astype(bf16)


def ffn_kernel(
    x_ref, g_ref, w_ref, back_ref, hidden_ref, grad_gate_ref, grad_up_ref, weights_ref
):
    for z in range(4):
        for xl in range(2):
            for xh in range(2):
                t = xl * 4 + z
                for k in range(3):
                    weights_ref[
                        k, xh * 176 : (xh + 1) * 176, t * 128 : (t + 1) * 128
                    ] = w_ref[z, xl, xh, k * 176 : (k + 1) * 176, :]

    def step(i, carry):
        rows = pl.ds(pl.multiple_of(i * 256, 256), 256)
        x, g = x_ref[rows, :], g_ref[rows, :]
        gate = dot_nt(x, weights_ref[0])
        up = dot_nt(x, weights_ref[1])
        grad_hidden = dot_nt(g, weights_ref[2])
        const = 0.7978845608028654
        inner = const * (gate + 0.044715 * gate * gate * gate)
        tanh = jnp.tanh(inner)
        gelu = 0.5 * gate * (1.0 + tanh)
        slope = 0.5 * (1.0 + tanh) + 0.5 * gate * (1.0 - tanh * tanh) * const * (
            1.0 + 3 * 0.044715 * gate * gate
        )
        hidden_ref[rows, :] = (gelu * up).astype(bf16)
        grad_gate = (grad_hidden * up * slope).astype(bf16)
        grad_up = (grad_hidden * gelu).astype(bf16)
        grad_gate_ref[rows, :] = grad_gate
        grad_up_ref[rows, :] = grad_up
        back = dot(grad_gate, weights_ref[0]) + dot(grad_up, weights_ref[1])
        back_ref[rows, :] = back.astype(bf16)
        return carry

    lax.fori_loop(0, 4, step, 0)


def ffn_out_kernel(hidden_ref, w_ref, out_ref):
    def step(i, carry):
        rows = pl.ds(pl.multiple_of(i * 256, 256), 256)
        out_ref[rows, :] = dot(hidden_ref[rows, :], w_ref[...]).astype(bf16)
        return carry

    lax.fori_loop(0, 4, step, 0)


def ffn_weights_kernel(x_ref, g_ref, hidden_ref, grad_gate_ref, grad_up_ref, out_ref):
    for t in range(8):
        xl, z = t // 4, t % 4
        cols = slice(t * 128, (t + 1) * 128)
        x, g = x_ref[:, cols], g_ref[:, cols]
        for k, (left, right) in enumerate(((grad_gate_ref, x), (grad_up_ref, x), (hidden_ref, g))):
            part = dot_tn(left[...], right).astype(bf16)
            for xh in range(2):
                out_ref[z, xl, xh, k * 176 : (k + 1) * 176, :] = part[
                    xh * 176 : (xh + 1) * 176
                ]


def middle_back_kernel(
    e_ref, cot_ref, after_cross_ref, after_self_ref, queries_ref, p_ref, kv_ref,
    gain_cross_ref, gain_ffn_ref, wo_ref, wcq_ref, wco_ref,
    att_ref, cross_branch_ref, grad_queries_ref, self_branch_ref, grad_kv_ref,
    grad_after_self_ref, gains_ref, grad_kv_packed_ref, grad_crossed_ref,
):
    grad_a, grad_gain = norm_back(after_cross_ref[...], gain_ffn_ref[...], e_ref[...])
    gains_ref[1:2, :] = grad_gain
    grad_after_cross = cot_ref[...].reshape(128, D).astype(f32) + grad_a
    branch = grad_after_cross.astype(bf16)
    cross_branch_ref[...] = branch
    grad_crossed_ref[...] = (
        dot_nt(branch[:, 0:HALF], wco_ref[0]) + dot_nt(branch[:, HALF:], wco_ref[1])
    ).astype(bf16)
    for mb in range(2):
        rows = slice(mb * 64, (mb + 1) * 64)
        for n in range(KV_HEADS):
            first = slice(2 * n * 64, (2 * n + 1) * 64)
            second = slice((2 * n + 1) * 64, (2 * n + 2) * 64)
            q = jnp.concatenate([queries_ref[rows, first], queries_ref[rows, second]], axis=0)
            go = jnp.concatenate(
                [grad_crossed_ref[rows, first], grad_crossed_ref[rows, second]], axis=0
            )
            kv = kv_ref[mb, n]
            p = p_ref[mb, n]
            wide = p.astype(f32)
            gp = dot_nt(go, kv[:, 64:128])
            centre = jnp.sum(wide * gp, axis=-1, keepdims=True)
            ds = (wide * (gp - centre)).astype(bf16)
            gq = (dot(ds, kv[:, 0:64]) * scaling).astype(bf16)
            grad_queries_ref[rows, first] = gq[0:64]
            grad_queries_ref[rows, second] = gq[64:128]
            gk = dot_tn(ds, q).astype(bf16)
            gv = dot_tn(p, go).astype(bf16)
            grad_kv_ref[mb, :, n * 64 : (n + 1) * 64] = gk
            grad_kv_ref[mb, :, HALF + n * 64 : HALF + (n + 1) * 64] = gv
    for mb in range(2):
        grad_kv_packed_ref[:, :, mb] = grad_kv_ref[mb].reshape(2, 8, 32, D)
    gq = grad_queries_ref[...]
    e = dot_nt(gq[:, 0:HALF], wcq_ref[0]) + dot_nt(gq[:, HALF:], wcq_ref[1])
    grad_a, grad_gain = norm_back(after_self_ref[...], gain_cross_ref[...], e)
    gains_ref[0:1, :] = grad_gain
    grad_after_self = grad_after_cross + grad_a
    grad_after_self_ref[...] = grad_after_self
    branch = grad_after_self.astype(bf16)
    self_branch_ref[...] = branch
    back = (dot_nt(branch[:, 0:HALF], wo_ref[0]) + dot_nt(branch[:, HALF:], wo_ref[1])).astype(bf16)
    for h in range(HEADS):
        one = back[:, h * 64 : (h + 1) * 64]
        att_ref[h] = jnp.concatenate([one[0:64], one[64:128]], axis=1)


def weights_kernel(
    attended_ref, self_branch_ref, normed_cross_ref, grad_queries_ref, crossed_ref,
    cross_branch_ref, mem_ref, grad_kv_ref, out_ref,
):
    for half in range(2):
        cols = slice(half * HALF, (half + 1) * HALF)
        out_ref[half, 0] = dot_tn(attended_ref[...], self_branch_ref[:, cols]).astype(bf16)
        out_ref[half, 1] = dot_tn(normed_cross_ref[...], grad_queries_ref[:, cols]).astype(bf16)
        out_ref[half, 3] = dot_tn(crossed_ref[...], cross_branch_ref[:, cols]).astype(bf16)
        total = None
        for mb in range(2):
            rows = mem_ref[:, :, mb].reshape(MEM, D)
            part = dot_tn(rows, grad_kv_ref[mb, :, cols])
            total = part if total is None else total + part
        out_ref[half, 2] = total.astype(bf16)


def last_kernel(
    back_ref, tok_ref, normed_ref, grad_after_self_ref, gain_ref, wq_ref, wkv_ref,
    grad_tok_ref, weights_ref, gain_out_ref, gq_ref, gk_ref, gv_ref,
):
    for h in range(HEADS):
        for mb in range(2):
            gq_ref[mb * 64 : (mb + 1) * 64, h * 64 : (h + 1) * 64] = back_ref[
                h, 0:64, mb * 64 : (mb + 1) * 64
            ]
    for n in range(KV_HEADS):
        both = back_ref[2 * n, 64:192, :].astype(f32) + back_ref[2 * n + 1, 64:192, :].astype(f32)
        both = both.astype(bf16)
        gk_ref[:, n * 64 : (n + 1) * 64] = both[:, 0:64]
        gv_ref[:, n * 64 : (n + 1) * 64] = both[:, 64:128]
    gq, gk, gv = gq_ref[...], gk_ref[...], gv_ref[...]
    e = dot_nt(gq[:, 0:HALF], wq_ref[0]) + dot_nt(gq[:, HALF:], wq_ref[1])
    e = e + dot_nt(gk, wkv_ref[0]) + dot_nt(gv, wkv_ref[1])
    x = tok_ref[...].reshape(128, D).astype(f32)
    grad_a, grad_gain = norm_back(x, gain_ref[...], e)
    gain_out_ref[...] = grad_gain
    grad_tok_ref[...] = (grad_after_self_ref[...] + grad_a).reshape(2, 64, D)
    normed = normed_ref[...]
    for half in range(2):
        cols = slice(half * HALF, (half + 1) * HALF)
        weights_ref[half, 0] = dot_tn(normed, gq[:, cols]).astype(bf16)
    weights_ref[0, 1] = dot_tn(normed, gk).astype(bf16)
    weights_ref[1, 1] = dot_tn(normed, gv).astype(bf16)


def on_device(
    tokens,
    memory,
    segment_ids,
    buckets,
    w_query,
    w_keyval,
    w_output,
    w_cross_query,
    w_cross_keyval,
    w_cross_output,
    norm_self,
    norm_cross,
    norm_ffn,
    bias_table,
    w_gate,
    w_up,
    w_down,
    cotangent,
):
    core = lax.axis_index("c")
    head = (lax.axis_index("y") * 2 + lax.axis_index("xh")) * 2 + core

    mem_chips = lax.all_gather(memory, ("y", "xh"), axis=0)
    mem_all = lax.all_gather(mem_chips, "c", axis=0)

    stacked = jnp.stack(
        [w_query, w_keyval, w_output, w_cross_query, w_cross_keyval, w_cross_output]
    )
    halves = jnp.moveaxis(stacked.reshape(6, 8, 2, HALF), 2, 0)
    rows = exchange(halves, "c")
    rows = jnp.moveaxis(rows, 0, 1).reshape(6, 16, HALF)

    ffn_rows = jnp.concatenate([w_gate.T, w_up.T, w_down], axis=0)
    later = jnp.concatenate([rows[2:].reshape(256, 128), ffn_rows], axis=0)
    along_x = to_all(later, ("xl", "xh"))

    small = jnp.concatenate([norm_self, norm_cross, norm_ffn, bias_table])
    small = jnp.pad(small, (0, 8 * HALF - small.shape[0])).reshape(8, HALF)
    first = jnp.concatenate([rows[0], rows[1], small], axis=0)
    first, along_x = lax.optimization_barrier((first, along_x))
    got = to_all(first, CHIPS)
    small = lax.all_gather(got[:, 32, 0:28], "c", axis=1).reshape(128, 28)
    gain_self = small[:, 0:8].reshape(1, D).astype(f32)
    gain_cross = small[:, 8:16].reshape(1, D).astype(f32)
    gain_ffn = small[:, 16:24].reshape(1, D).astype(f32)
    table = small[:, 24:28].reshape(HEADS, BUCKETS)
    table = lax.dynamic_slice_in_dim(table, head, 1, 0).astype(f32).reshape(BUCKETS, 1)
    pair = jnp.stack([got[:, 0:16].reshape(D, HALF), got[:, 16:32].reshape(D, HALF)])
    pair = lax.all_gather(pair, "c", axis=0)
    wq, wkv = pair[:, 0], pair[:, 1]

    other = lax.all_gather(along_x[:, 0:256], ("z", "y"), axis=0)
    other = other.reshape(4, 4, 2, 2, 4, 16, HALF)
    other = other.transpose(4, 2, 0, 1, 3, 5, 6).reshape(4, D, HALF)
    other = lax.all_gather(other, "c", axis=0)
    wo, wcq, wckv, wco = (other[:, k] for k in range(4))

    ffn_w = lax.all_gather(along_x[:, 256:], "z", axis=0).reshape(4, 2, 2, 528, 128)
    cot_all = lax.all_gather(cotangent.reshape(128, D), ("c", "y"), axis=0).reshape(1024, D)

    packed, normed_self = call(
        project_kernel,
        (((16, 192, 128), bf16), ((128, D), bf16)),
        tokens, gain_self, wq, wkv,
    )
    qkv = exchange(packed, FFN)
    turned = jnp.roll(buckets[::-1], 1).reshape(1, SEQ)
    att, o_self, p_self = call(
        self_kernel,
        (((16, 64, 128), bf16), ((SEQ, 128), f32), ((2, SEQ, SEQ), bf16)),
        qkv, table, turned, segment_ids, segment_ids.reshape(2, SEQ, 1),
    )
    att = exchange(att, FFN)

    (kv_mem,) = call(memory_kernel, (((2, 8, MEM, 128), bf16),), mem_all, wckv)
    (
        attended, after_self, normed_cross, queries, p_cross, crossed, after_cross, normed_ffn,
    ) = call(
        middle_kernel,
        (
            ((128, D), bf16), ((128, D), f32), ((128, D), bf16), ((128, D), bf16),
            ((2, 8, 128, MEM), bf16), ((128, D), bf16), ((128, D), f32), ((128, D), bf16),
        ),
        att, tokens, gain_cross, gain_ffn, wo, wcq, wco, kv_mem,
    )

    normed_all = lax.all_gather(to_all(normed_ffn, "y"), "c", axis=0).reshape(1024, D)
    back, hidden, grad_gate, grad_up, ffn_used = call(
        ffn_kernel,
        (
            ((1024, D), bf16), ((1024, 352), bf16), ((1024, 352), bf16), ((1024, 352), bf16),
            ((3, 352, D), bf16),
        ),
        normed_all, cot_all, ffn_w,
    )
    back = back.reshape(2, 4, 128, D)
    mine = lax.dynamic_index_in_dim(back, core, 0, keepdims=False)
    theirs = lax.dynamic_index_in_dim(back, 1 - core, 0, keepdims=False)
    back = (mine.astype(f32) + swap_core(theirs).astype(f32)).astype(bf16)
    grad_normed_ffn = sum_of_all(back, "y")

    (out_part,) = call(ffn_out_kernel, (((1024, D), bf16),), hidden, ffn_used[2])
    out = lax.psum_scatter(out_part, ("c", "y"), scatter_dimension=0, tiled=True)
    output = (after_cross + out.astype(f32)).reshape(2, 64, D)
    (ffn_grads,) = call(
        ffn_weights_kernel,
        (((4, 2, 2, 528, 128), bf16),),
        normed_all, cot_all, hidden, grad_gate, grad_up,
    )
    ffn_grads = lax.psum_scatter(
        ffn_grads.reshape(4 * 2112, 128), "z", scatter_dimension=0, tiled=True
    )

    (
        att, cross_branch, grad_queries, self_branch, grad_kv, grad_after_self, gain_grads,
        grad_kv_packed,
    ) = call(
        middle_back_kernel,
        (
            ((16, 64, 128), bf16), ((128, D), bf16), ((128, D), bf16), ((128, D), bf16),
            ((2, MEM, D), bf16), ((128, D), f32), ((2, D), f32), ((2, 8, 2, 32, D), bf16),
        ),
        grad_normed_ffn, cotangent, after_cross, after_self, queries, p_cross, kv_mem,
        gain_cross, gain_ffn, wo, wcq, wco,
        scratch=[pltpu.VMEM((128, D), bf16)],
    )
    go = exchange(att, FFN)

    back, grad_table = call(
        self_back_kernel,
        (((16, 192, 128), bf16), ((BUCKETS, 1), f32)),
        qkv, go, o_self, p_self, turned,
        scratch=[pltpu.VMEM((4, BLOCK, BLOCK), f32)],
    )
    back = exchange(back, FFN)
    grad_tokens, grads_first, gain_grad_self = call(
        last_kernel,
        (((2, 64, D), f32), ((2, 2, D, HALF), bf16), ((1, D), f32)),
        back, tokens, normed_self, grad_after_self, gain_self, wq, wkv,
        scratch=[pltpu.VMEM((128, D), bf16), pltpu.VMEM((128, HALF), bf16),
                 pltpu.VMEM((128, HALF), bf16)],
    )

    mine = lax.dynamic_index_in_dim(grad_kv_packed, core, 0, keepdims=False)
    theirs = lax.dynamic_index_in_dim(grad_kv_packed, 1 - core, 0, keepdims=False)
    grad_mem = (mine.astype(f32) + swap_core(theirs).astype(f32)).astype(bf16)
    grad_mem = lax.psum_scatter(
        grad_mem.reshape(8 * 64, D), ("y", "xh"), scatter_dimension=0, tiled=True
    )
    grad_memory = dot_nt(grad_mem[:, 0:HALF], wckv[0]) + dot_nt(grad_mem[:, HALF:], wckv[1])
    grad_memory = grad_memory.reshape(2, 32, D)

    (grads_other,) = call(
        weights_kernel,
        (((2, 4, D, HALF), bf16),),
        attended, self_branch, normed_cross, grad_queries, crossed, cross_branch, mem_all, grad_kv,
    )
    mine = lax.dynamic_index_in_dim(grads_other, core, 0, keepdims=False)
    theirs = lax.dynamic_index_in_dim(grads_other, 1 - core, 0, keepdims=False)
    both = (mine.astype(f32) + swap_core(theirs).astype(f32)).astype(bf16)
    both = both.reshape(4, 2, 4, 4, 2, 16, HALF)
    both = both.transpose(2, 3, 1, 4, 0, 5, 6).reshape(16 * 256, HALF)
    both = lax.psum_scatter(both, ("z", "y"), scatter_dimension=0, tiled=True)

    tail_x = jnp.concatenate(
        [both.reshape(4, 256, 128), ffn_grads.reshape(4, 528, 128)], axis=1
    )
    tail_x = sum_of_all(tail_x, ("xl", "xh"))
    rows_other = tail_x[0:256].reshape(4, 16, HALF)
    ffn_final = tail_x[256:]

    mine = lax.dynamic_index_in_dim(grads_first, core, 0, keepdims=False)
    theirs = lax.dynamic_index_in_dim(grads_first, 1 - core, 0, keepdims=False)
    both = (mine.astype(f32) + swap_core(theirs).astype(f32)).astype(bf16)
    both = both.reshape(2, 64, 16, HALF).transpose(1, 0, 2, 3).reshape(64, 32, HALF)
    table_all = jnp.where(
        jnp.arange(HEADS)[:, None] == head, grad_table.reshape(1, BUCKETS), 0.0
    ).reshape(64, 8)
    gains = jnp.concatenate([gain_grad_self, gain_grads], axis=0)
    gains = gains.reshape(3, 64, 16).transpose(1, 0, 2).reshape(64, 48)
    small = jnp.concatenate([gains, table_all], axis=1)
    small = small + swap_core(small)
    small = jnp.pad(small.astype(bf16), ((0, 0), (0, 8 * HALF - 56))).reshape(64, 8, HALF)
    first = sum_of_all(jnp.concatenate([both, small], axis=1), CHIPS)
    rows_first = first[0:32].reshape(2, 16, HALF)
    small = first[32, 0:56]

    rows = jnp.concatenate([rows_first, rows_other], axis=0)
    rows = exchange(jnp.moveaxis(rows.reshape(6, 2, 8, HALF), 1, 0), "c")
    rows = jnp.moveaxis(rows, 0, 2).reshape(6, 8, D)

    gains = small[0:48].reshape(3, 2, 8)
    gains = lax.dynamic_index_in_dim(gains, core, 1, keepdims=False)
    table_grad = lax.dynamic_index_in_dim(small[48:56].reshape(2, 4), core, 0, keepdims=False)
    return (
        output,
        grad_tokens,
        grad_memory,
        rows[0],
        rows[1],
        rows[2],
        rows[3],
        rows[4],
        rows[5],
        gains[0],
        gains[1],
        gains[2],
        table_grad,
        ffn_final[0:176].T,
        ffn_final[176:352].T,
        ffn_final[352:528],
    )


def solution(mesh):
    names = Mesh(mesh.devices.reshape(2, 4, 4, 2, 2), EVERY)
    tok, ffn, both = ("xl", "z"), FFN, EVERY
    big, mat, vec = P(None, both, None), P(both, None), P(both)
    fn = jax.shard_map(
        on_device,
        mesh=names,
        in_specs=(
            big, big, P(None, tok), P(), mat, mat, mat, mat, mat, mat, vec, vec, vec, vec,
            P(tok, ffn), P(tok, ffn), P(ffn, tok), big,
        ),
        out_specs=(
            big, big, big, mat, mat, mat, mat, mat, mat, vec, vec, vec, vec,
            P(tok, ffn), P(tok, ffn), P(ffn, tok),
        ),
        check_vma=False,
    )
    return fn
```

time: 1580 us -> 628 us (0.40)
  local copies, waits for them, and re-layouts: 692 us -> 69.5 us
  waiting for transfers between devices: 567 us -> 303 us
  matrix products: 194 us -> 4.15 us
  blocking collectives: 0 us -> 90.3 us
  other arithmetic: 98 us -> 21 us
  Pallas kernels: 0 us -> 75.9 us
  starting transfers between devices: 0.86 us -> 39.8 us
    unnamed x15 -> x12, waiting for transfers between devices: 498 us -> 1.38 us
    gather x2 -> x0, local copies, waits for them, and re-layouts: 261 us -> none  [on_device(): bucket_row_indices = buckets[distance]]
    dot_general x75 -> x2, matrix products: 194 us -> 4.15 us  [dot_nt(): lax.dot_general(a, b, (((1,), (1,)), ((), ())), preferred_element_type=f32)]
    all_gather x4 -> x8, waiting for transfers between devices: 0.03 us -> 107 us  [the longest x1 34.2 us: on_device(): mem_chips = lax.all_gather(memory, ('y', 'xh'), axis=0)]
    another operation x28 -> x1, local copies, waits for them, and re-layouts: 104 us -> 0.72 us  [on_device(): jnp.stack([w_query, w_keyval, w_output, w_cross_query, w_cross_keyval, w_...]
    all_to_all x0 -> x6, blocking collectives: none -> 86.7 us  [the longest x5 68.3 us: exchange(): return lax.all_to_all(x, axes, 0, 0, tiled=True)]
    unnamed x368 -> x101, local copies, waits for them, and re-layouts: 99.4 us -> 20.7 us
    pallas_call x0 -> x11, Pallas kernels: none -> 75.9 us  [call(): pl.pallas_call(kernel, out_shape=tuple((jax.ShapeDtypeStruct(s, t) for s,...]
  transfers between devices with their start and end apart: 12 -> 23, of which waited for: 3 -> 13; matrix products, arithmetic and copies ran while one was open for 52% -> 11% of each run, Pallas kernels for 0% -> 11%
where the time goes in v1:
time: 628 us; the launch traced here: 619 us
  waiting for transfers between devices  303 us (48%)
  blocking collectives  90.3 us (14%)
  Pallas kernels  75.9 us (12%)
  local copies, waits for them, and re-layouts  69.5 us (11%)
  starting transfers between devices  39.8 us (6%)
  other arithmetic  21 us (3%)
  between operations  15.4 us (2%)
    reduce_scatter x1, waiting for transfers between devices, on_device(): both = lax.psum_scatter(both, ('z', 'y'), scatter_dimension=0, tiled=True)  87 us
    pallas_call x11, Pallas kernels, call(): pl.pallas_call(kernel, out_shape=tuple((jax.ShapeDtypeStruct(s, t) for s,...  75.9 us
    all_to_all x5, blocking collectives, exchange(): return lax.all_to_all(x, axes, 0, 0, tiled=True)  68.3 us
    all_to_all x2, waiting for transfers between devices, to_all(): lax.all_to_all(jnp.broadcast_to(x[None], (n, *x.shape)), axes, 0, 0, tile...  44.1 us
    all_gather x1, waiting for transfers between devices, on_device(): mem_chips = lax.all_gather(memory, ('y', 'xh'), axis=0)  34.2 us
    reduce_scatter x1, waiting for transfers between devices, on_device(): lax.psum_scatter(ffn_grads.reshape(4 * 2112, 128), 'z', scatter_dimension...  32.5 us
    all_gather x1, waiting for transfers between devices, on_device(): other = lax.all_gather(along_x[:, 0:256], ('z', 'y'), axis=0)  31.8 us
    all_to_all x4, waiting for transfers between devices, exchange(): return lax.all_to_all(x, axes, 0, 0, tiled=True)  21.8 us
  transfers between devices with their start and end apart: 23, of which 13 were waited for; matrix products, arithmetic and copies ran while one was open for 11% of the time, Pallas kernels for 11%

profile of v1, /device:TPU:1, one launch (start us, length us, event | category | flops | bytes accessed | tf_op | source)
XLA Modules:
  0.0 619.2 jit_solution(1607213259842142165)
XLA Ops:
  11.6 4.9 all_to_all.60
  22.6 12.2 %all-to-all-done.1 = bf16[4,784,128]{2,1,0:T(8,128)(2,1)S(1)} async-done(((bf16[4,784,128]{2,1,0:T(8,128)(2,1)}), bf16[4,784,128]{2,1,0:T(8,128)(2,1)S(1)}, u32[]{:S(2)}, u32[]{:S(2)}) %all-to-all-start.1) | async-done | bytes 802848 | tf_op jit(solution)/shard_map/all_to_all | solution.py:66
  37.2 9.0 %all-to-all-start.2 = ((bf16[64,40,512]{2,1,0:T(8,128)(2,1)}), bf16[64,40,512]{2,1,0:T(8,128)(2,1)S(1)}, u32[]{:S(2)}, u32[]{:S(2)}) async-start(bf16[64,40,512]{2,1,0:T(8,128)(2,1)} %broadcast_in_dim.48), calls=%async_computation.2 | async-start | bytes 5242880 | tf_op jit(solution)/shard_map/all_to_all | solution.py:66
  47.0 32.0 %all-to-all-done.2 = bf16[64,40,512]{2,1,0:T(8,128)(2,1)S(1)} async-done(((bf16[64,40,512]{2,1,0:T(8,128)(2,1)}), bf16[64,40,512]{2,1,0:T(8,128)(2,1)S(1)}, u32[]{:S(2)}, u32[]{:S(2)}) %all-to-all-start.2) | async-done | bytes 2621472 | tf_op jit(solution)/shard_map/all_to_all | solution.py:66
  80.8 31.8 %all-gather.21.cloned.1.call-done = bf16[64,256,128]{2,1,0:T(8,128)(2,1)} async-done(((bf16[4,256,128]{2,1,0:T(8,128)(2,1)}), bf16[64,256,128]{2,1,0:T(8,128)(2,1)}) %all-gather.21.cloned.1.call-update) | async-done | bytes 4194320 | tf_op jit(solution)/shard_map/all_gather | solution.py:445
  112.7 7.6 %reshape.245 = bf16[4,4,2,2,4,16,512]{6,5,4,3,2,1,0:T(8,128)(2,1)} reshape(bf16[64,256,128]{2,1,0:T(8,128)(2,1)} %all-gather.21.cloned.1.call-done) | data formatting | bytes 8388608 | tf_op jit(solution)/shard_map/reshape | solution.py:446
  120.2 4.9 copy.72
  125.2 34.2 %all-gather.23.cloned.1.call-done = bf16[16,32,1024]{2,1,0:T(8,128)(2,1)} async-done(((bf16[2,32,1024]{2,1,0:T(8,128)(2,1)}), bf16[16,32,1024]{2,1,0:T(8,128)(2,1)}) %all-gather.23.cloned.1.call-update) | async-done | bytes 1048592 | tf_op jit(solution)/shard_map/all_gather | solution.py:416
  165.0 13.2 %all-gather.19.cloned.1.call-done = bf16[4,1024,512]{2,1,0:T(8,128)(2,1)} async-done(((bf16[2,1024,512]{2,1,0:T(8,128)(2,1)}), bf16[4,1024,512]{2,1,0:T(8,128)(2,1)}) %all-gather.19.cloned.1.call-update) | async-done | bytes 4194320 | tf_op jit(solution)/shard_map/all_gather | solution.py:442
  183.8 7.0 %all-to-all-start.3 = ((bf16[16,192,128]{2,1,0:T(8,128)(2,1)}), bf16[16,192,128]{2,1,0:T(8,128)(2,1)S(1)}, u32[]{:S(2)}, u32[]{:S(2)}) async-start(bf16[16,192,128]{2,1,0:T(8,128)(2,1)} %copy-done.21), calls=%async_computation.3 | async-start | bytes 1572864 | tf_op jit(solution)/shard_map/all_to_all | solution.py:70
  194.2 11.1 %all-to-all-done.3.qkv_ref = bf16[16,192,128]{2,1,0:T(8,128)(2,1)S(1)} async-done(((bf16[16,192,128]{2,1,0:T(8,128)(2,1)}), bf16[16,192,128]{2,1,0:T(8,128)(2,1)S(1)}, u32[]{:S(2)}, u32[]{:S(2)}) %all-to-all-start.3) | async-done | bytes 786464 | tf_op jit(solution)/shard_map/all_to_all | solution.py:70
  206.5 7.3 %shard_map.298 = (bf16[16,64,128]{2,1,0:T(8,128)(2,1)S(1)}, f32[1024,128]{1,0:T(8,128)S(1)}, bf16[2,1024,1024]{2,1,0:T(8,128)(2,1)}) custom-call(bf16[16,192,128]{2,1,0:T(8,128)(2,1)S(1)} %all-to-all-done.3.qkv_ref, f32[32,1]{1,0:T(8,128)S(1)} %copy.70.table_ref, s32[1,1024]{1,0:T(1,128)S(1)} %bitcast.127, s32[2,1024]{1,0:T(2,128)S(1)} %copy-done.39, ...), custom_call_target="tpu_custom_call" | custom-call | tf_op jit(solution)/shard_map/pallas_call | solution.py:56
  220.0 6.0 slice_bitcast_fusion
  233.0 11.0 %shard_map.300 = (bf16[128,1024]{1,0:T(8,128)(2,1)S(1)}, f32[128,1024]{1,0:T(8,128)S(1)}, bf16[128,1024]{1,0:T(8,128)(2,1)S(1)}, bf16[128,1024]{1,0:T(8,128)(2,1...) custom-call(bf16[16,64,128]{2,1,0:T(8,128)(2,1)S(1)} %all-to-all-don, ...), custom_call_target="tpu_custom_call" | custom-call | tf_op jit(solution)/shard_map/pallas_call | solution.py:56
  249.8 18.5 %all_to_all.61 = bf16[4,128,1024]{2,1,0:T(8,128)(2,1)} all-to-all(bf16[4,128,1024]{2,1,0:T(8,128)(2,1)S(1)} %broadcast_in_dim.49), channel_id=1, replica_groups=mesh['xl'=2,'z'=4,'y'=4,'xh'=2,'c'=2] {'y'}, dimensions={0} | all-to-all | bytes 2097152 | tf_op jit(solution)/shard_map/all_to_all | solution.py:66
  268.4 12.7 %all-gather.29.cloned.1.call-done = bf16[16,528,128]{2,1,0:T(8,128)(2,1)} async-done(((bf16[4,528,128]{2,1,0:T(8,128)(2,1)}), bf16[16,528,128]{2,1,0:T(8,128)(2,1)}) %all-gather.29.cloned.1.call-update) | async-done | bytes 2162704 | tf_op jit(solution)/shard_map/all_gather | solution.py:451
  281.1 15.3 %all-gather.27.cloned.1.call-done = bf16[8,128,1024]{2,1,0:T(8,128)(2,1)} async-done(((bf16[4,128,1024]{2,1,0:T(8,128)(2,1)}), bf16[8,128,1024]{2,1,0:T(8,128)(2,1)}) %all-gather.27.cloned.1.call-update) | async-done | bytes 2097168 | tf_op jit(solution)/shard_map/all_gather | solution.py:480
  296.3 9.9 %shard_map.301 = (bf16[1024,1024]{1,0:T(8,128)(2,1)S(1)}, bf16[1024,352]{1,0:T(8,128)(2,1)S(1)}, bf16[1024,352]{1,0:T(8,128)(2,1)S(1)}, bf16[1024,352]{1,0:T(8,128)(2,1)S(1)}, bf16[3,352,1024]{2,1,0:T(8,128)(2,1)}) custom-call(bf16[1024,1024]{1,0:T(8,128)(2,1)} %bitcast.122, bf16[1024,1024]{1,0:T(8,128)(2,1)} %bitcast.136, bf16[4,2,2,528,128]{4,3,2,1,0:T(8,128)(2,1)} %bitcast.144), custom_call_target="tpu_custom_call" | custom-call | tf_op jit(solution)/shard_map/pallas_call | solution.py:56
  314.5 25.7 %all_to_all.62 = bf16[4,128,1024]{2,1,0:T(8,128)(2,1)S(1)} all-to-all(bf16[4,128,1024]{2,1,0:T(8,128)(2,1)S(1)} %fusion.3), channel_id=1, replica_groups=mesh['xl'=2,'z'=4,'y'=4,'xh'=2,'c'=2] {'y'}, dimensions={0} | all-to-all | bytes 2097152 | tf_op jit(solution)/shard_map/all_to_all | solution.py:70
  340.5 14.1 %shard_map.303 = (bf16[16,64,128]{2,1,0:T(8,128)(2,1)S(1)}, bf16[128,1024]{1,0:T(8,128)(2,1)S(1)}, bf16[128,1024]{1,0:T(8,128)(2,1)S(1)}, bf16[128,1024]{1,0:T(8...) custom-call(f32[128,1024]{1,0:T(8,128)S(1)} %convert_reduce_fusion.1, ...), custom_call_target="tpu_custom_call" | custom-call | tf_op jit(solution)/shard_map/pallas_call | solution.py:56
  354.6 7.3 %shard_map.306 = bf16[2,4,1024,512]{3,2,1,0:T(8,128)(2,1)} custom-call(bf16[128,1024]{1,0:T(8,128)(2,1)S(1)} %copy-done.29, bf16[128,1024]{1,0:T(8,128)(2,1)S(1)} %get-tuple-element.74.self_branch_ref, bf16[128,1024]{1,0:T(8,128)(2,1)S(1)} %copy-done.31, bf16[128,1024]{1,0:T(8,128)(2,1)S(1)} %get-tuple-element.76.grad_queries_ref, ...), custom_call_target="tpu_custom_call" | custom-call | tf_op jit(solution)/shard_map/pallas_call | solution.py:56
  361.9 4.7 dynamic-slice_bitcast_fusion
  369.8 8.0 %collective-permute-done.1 = bf16[8,2,32,1024]{3,2,1,0:T(8,128)(2,1)S(1)} collective-permute-done((bf16[8,2,32,1024]{3,2,1,0:T(8,128)(2,1)S(1)}, bf16[8,2,32,1024]{3,2,1,0:T(8,128)(2,1)S(1)}, u32[]{:S(2)}, u32[]{:S(2)}) %collective-permute-start.1) | collective-permute-done | bytes 1048608 | tf_op jit(solution)/shard_map/ppermute | solution.py:78
  379.4 4.7 fusion
  386.7 13.8 %all_to_all.63.go_ref = bf16[16,64,128]{2,1,0:T(8,128)(2,1)S(1)} all-to-all(bf16[16,64,128]{2,1,0:T(8,128)(2,1)S(1)} %get-tuple-element.61), channel_id=1, replica_groups=mesh['xl'=2,'z'=4,'y'=4,'xh'=2,'c'=2] {'y','xh','c'}, dimensions={0} | all-to-all | bytes 524288 | tf_op jit(solution)/shard_map/all_to_all | solution.py:70
  401.6 6.6 %shard_map.304 = (bf16[16,192,128]{2,1,0:T(8,128)(2,1)S(1)}, f32[32,1]{1,0:T(8,128)S(1)}) custom-call(bf16[16,192,128]{2,1,0:T(8,128)(2,1)S(1)} %all-to-all-done.3.qkv_ref, bf16[16,64,128]{2,1,0:T(8,128)(2,1)S(1)} %all_to_all.63.go_ref, f32[1024,128]{1,0:T(8,128)S(1)} %copy-done.23, bf16[2,1024,1024]{2,1,0:T(8,128)(2,1)} %get-tuple-element.63.p_ref, ...), custom_call_target="tpu_custom_call" | custom-call | tf_op jit(solution)/shard_map/pallas_call | solution.py:56
  408.2 19.6 %all_to_all.64.back_ref = bf16[16,192,128]{2,1,0:T(8,128)(2,1)S(1)} all-to-all(bf16[16,192,128]{2,1,0:T(8,128)(2,1)S(1)} %get-tuple-element.64), channel_id=1, replica_groups=mesh['xl'=2,'z'=4,'y'=4,'xh'=2,'c'=2] {'y','xh','c'}, dimensions={0} | all-to-all | bytes 1572864 | tf_op jit(solution)/shard_map/all_to_all | solution.py:70
  436.9 8.3 %shard_map.307 = bf16[4,2,2,528,128]{4,3,2,1,0:T(8,128)(2,1)} custom-call(bf16[1024,1024]{1,0:T(8,128)(2,1)S(1)} %bitcast.123, bf16[1024,1024]{1,0:T(8,128)(2,1)} %bitcast.137, bf16[1024,352]{1,0:T(8,128)(2,1)S(1)} %copy-done.9, bf16[1024,352]{1,0:T(8,128)(2,1)S(1)} %copy-done.18, bf16[1024,352]{1,0:T(8,128)(2,1)S(1)} %copy-done.20), custom_call_target="tpu_custom_call" | custom-call | tf_op jit(solution)/shard_map/pallas_call | solution.py:56
  453.9 5.7 all-to-all-start.9
  465.6 87.0 %reduce-scatter.9.cloned.1.call-done = bf16[256,512]{1,0:T(8,128)(2,1)} async-done(((bf16[4096,512]{1,0:T(8,128)(2,1)}), bf16[256,512]{1,0:T(8,128)(2,1)}) %reduce-scatter.9.cloned.1.call-update) | async-done | bytes 262160 | tf_op jit(solution)/shard_map/reduce_scatter | solution.py:556
  553.7 32.5 %reduce-scatter.11.cloned.1.call-done = bf16[2112,128]{1,0:T(8,128)(2,1)} async-done(((bf16[8448,128]{1,0:T(8,128)(2,1)}), bf16[2112,128]{1,0:T(8,128)(2,1)}) %reduce-scatter.11.cloned.1.call-update) | async-done | bytes 540688 | tf_op jit(solution)/shard_map/reduce_scatter | solution.py:503
  594.2 10.7 %all-to-all-done.10 = bf16[4,784,128]{2,1,0:T(8,128)(2,1)} async-done(((bf16[4,784,128]{2,1,0:T(8,128)(2,1)}), bf16[4,784,128]{2,1,0:T(8,128)(2,1)}, u32[]{:S(2)}, u32[]{:S(2)}) %all-to-all-start.10) | async-done | bytes 802848 | tf_op jit(solution)/shard_map/all_to_all | solution.py:70
  (228 shorter events, 106.7 us)
Async XLA Ops:
  7.2 15.3 %copy-start.43 = (bf16[4]{0:T(256)(128)(2,1)S(1)}, bf16[4]{0:T(256)(128)(2,1)}, u32[]{:S(2)}) copy-start(bf16[4]{0:T(256)(128)(2,1)} %param.31) | copy-start | bytes 28
  7.2 15.3 %copy-start.44 = (bf16[8]{0:T(256)(128)(2,1)S(1)}, bf16[8]{0:T(256)(128)(2,1)}, u32[]{:S(2)}) copy-start(bf16[8]{0:T(256)(128)(2,1)} %param.30) | copy-start | bytes 52
  18.4 16.4 %all-to-all-start.1 = ((bf16[4,784,128]{2,1,0:T(8,128)(2,1)}), bf16[4,784,128]{2,1,0:T(8,128)(2,1)S(1)}, u32[]{:S(2)}, u32[]{:S(2)}) async-start(bf16[4,784,128]{2,1,0:T(8,128)(2,1)} %broadcast_in_dim.47), calls=%async_computation.1 | async-start | bytes 1605632 | tf_op jit(solution)/shard_map/all_to_all | solution.py:66
  22.5 90.2 %all-gather.21.cloned.1.call-start = ((), (), s32[]{:S(2)}) async-start(), calls=%async_computation.23 | async-start | bytes 4456448 | tf_op jit(solution)/shard_map/all_gather | solution.py:445
  37.2 41.8 %all-to-all-start.2 = ((bf16[64,40,512]{2,1,0:T(8,128)(2,1)}), bf16[64,40,512]{2,1,0:T(8,128)(2,1)S(1)}, u32[]{:S(2)}, u32[]{:S(2)}) async-start(bf16[64,40,512]{2,1,0:T(8,128)(2,1)} %broadcast_in_dim.48), calls=%async_computation.2 | async-start | bytes 5242880 | tf_op jit(solution)/shard_map/all_to_all | solution.py:66
  46.2 113.3 %all-gather.23.cloned.1.call-start = ((), (), s32[]{:S(2)}) async-start(), calls=%async_computation.24 | async-start | bytes 1179648 | tf_op jit(solution)/shard_map/all_gather | solution.py:416
  46.9 131.3 %all-gather.19.cloned.1.call-start = ((), (), s32[]{:S(2)}) async-start(), calls=%async_computation.22 | async-start | bytes 6291456 | tf_op jit(solution)/shard_map/all_gather | solution.py:442
  80.8 139.2 %all-gather.15.cloned.1.call-start = ((), (), s32[]{:S(2)}) async-start(), calls=%async_computation.16 | async-start | bytes 12582912 | tf_op jit(solution)/shard_map/all_gather | solution.py:448
  125.2 100.9 %all-gather.25.cloned.1.call-start = ((), (), s32[]{:S(2)}) async-start(), calls=%async_computation.25 | async-start | bytes 3145728 | tf_op jit(solution)/shard_map/all_gather | solution.py:417
  159.5 108.9 %all-gather.17.cloned.1.call-start = ((), (), s32[]{:S(2)}) async-start(), calls=%async_computation.17 | async-start | bytes 2359296 | tf_op jit(solution)/shard_map/all_gather | solution.py:452
  160.0 121.0 %all-gather.29.cloned.1.call-start = ((), (), s32[]{:S(2)}) async-start(), calls=%async_computation.27 | async-start | bytes 2703360 | tf_op jit(solution)/shard_map/all_gather | solution.py:451
  183.8 21.4 %all-to-all-start.3 = ((bf16[16,192,128]{2,1,0:T(8,128)(2,1)}), bf16[16,192,128]{2,1,0:T(8,128)(2,1)S(1)}, u32[]{:S(2)}, u32[]{:S(2)}) async-start(bf16[16,192,128]{2,1,0:T(8,128)(2,1)} %copy-done.21), calls=%async_computation.3 | async-start | bytes 1572864 | tf_op jit(solution)/shard_map/all_to_all | solution.py:70
  215.3 17.7 %all-to-all-start.4 = ((bf16[16,64,128]{2,1,0:T(8,128)(2,1)}), bf16[16,64,128]{2,1,0:T(8,128)(2,1)S(1)}, u32[]{:S(2)}, u32[]{:S(2)}) async-start(bf16[16,64,128]{2,1,0:T(8,128)(2,1)} %copy-done.38), calls=%async_computation.4 | async-start | bytes 524288 | tf_op jit(solution)/shard_map/all_to_all | solution.py:70
  219.5 76.9 %all-gather.27.cloned.1.call-start = ((), (), s32[]{:S(2)}) async-start(), calls=%async_computation.26 | async-start | bytes 3145728 | tf_op jit(solution)/shard_map/all_gather | solution.py:480
  268.3 191.3 %reduce-scatter.5.cloned.1.call-start = ((), (), s32[]{:S(2)}) async-start(), calls=%async_computation.18 | async-start | bytes 2359296 | tf_op jit(solution)/shard_map/reduce_scatter | solution.py:496
  307.5 4.9 collective-permute-start
  312.4 149.0 %reduce-scatter.7.cloned.1.call-start = ((), (), s32[]{:S(2)}) async-start(), calls=%async_computation.19 | async-start | bytes 1179648 | tf_op jit(solution)/shard_map/reduce_scatter | solution.py:540
  314.4 26.0 %copy-start.14 = (f32[128,1024]{1,0:T(8,128)S(1)}, f32[128,1024]{1,0:T(8,128)}, u32[]{:S(2)}) copy-start(f32[128,1024]{1,0:T(8,128)} %copy-done.13) | copy-start | bytes 1572868
  314.4 26.0 %copy-start.16 = (bf16[2,64,1024]{2,1,0:T(8,128)(2,1)S(1)}, bf16[2,64,1024]{2,1,0:T(8,128)(2,1)}, u32[]{:S(2)}) copy-start(bf16[2,64,1024]{2,1,0:T(8,128)(2,1)} %cot_ref.1) | copy-start | bytes 786436
  314.5 26.0 %copy-start.27 = (f32[128,1024]{1,0:T(8,128)S(1)}, f32[128,1024]{1,0:T(8,128)}, u32[]{:S(2)}) copy-start(f32[128,1024]{1,0:T(8,128)} %copy-done.26) | copy-start | bytes 1572868
  314.5 25.9 %copy-start.37 = (bf16[128,1024]{1,0:T(8,128)(2,1)S(1)}, bf16[128,1024]{1,0:T(8,128)(2,1)}, u32[]{:S(2)}) copy-start(bf16[128,1024]{1,0:T(8,128)(2,1)} %copy-done.36) | copy-start | bytes 786436
  366.6 12.8 %collective-permute-start.4 = (bf16[4,1024,512]{2,1,0:T(8,128)(2,1)}, bf16[4,1024,512]{2,1,0:T(8,128)(2,1)}, u32[]{:S(2)}, u32[]{:S(2)}) collective-permute-start(bf16[4,1024,512]{2,1,0:T(8,128)(2,1)} %dynamic-slice_bitcast_fusion), channel_id=1, source_target_pairs={{0,1},{1,0},{2,3},{3,2},{4,5},{5,4},{6,7},{7,6},{8,9},{9,8},{10,11... | collective-permute-start | bytes 12582920 | tf_op jit(solution)/shard_map/ppermute | solution.py:78
  369.7 8.1 %collective-permute-start.1 = (bf16[8,2,32,1024]{3,2,1,0:T(8,128)(2,1)S(1)}, bf16[8,2,32,1024]{3,2,1,0:T(8,128)(2,1)S(1)}, u32[]{:S(2)}, u32[]{:S(2)}) collective-permute-start(bf16[8,2,32,1024]{3,2,1,0:T(8,128)(2,1)S(1)} %dynamic-slice_bitcast_fusion.2), channel_id=1, source_target_pairs={{0,1},{1,0},{2,3},{3,2},{4,5},{5,4},{6,7},{7,6},{8,9},{9,8},{10,11... | collective-permute-start | bytes 3145736 | tf_op jit(solution)/shard_map/ppermute | solution.py:78
  379.1 173.5 %reduce-scatter.9.cloned.1.call-start = ((), (), s32[]{:S(2)}) async-start(), calls=%async_computation.20 | async-start | bytes 4456448 | tf_op jit(solution)/shard_map/reduce_scatter | solution.py:556
  386.7 199.5 %reduce-scatter.11.cloned.1.call-start = ((), (), s32[]{:S(2)}) async-start(), calls=%async_computation.21 | async-start | bytes 2703360 | tf_op jit(solution)/shard_map/reduce_scatter | solution.py:503
  401.6 26.2 %copy-start.2 = (bf16[2,1024,512]{2,1,0:T(8,128)(2,1)S(1)}, bf16[2,1024,512]{2,1,0:T(8,128)(2,1)}, u32[]{:S(2)}) copy-start(bf16[2,1024,512]{2,1,0:T(8,128)(2,1)} %copy-done.1) | copy-start | bytes 6291460
  401.6 26.2 %copy-start.25 = (f32[128,1024]{1,0:T(8,128)S(1)}, f32[128,1024]{1,0:T(8,128)}, u32[]{:S(2)}) copy-start(f32[128,1024]{1,0:T(8,128)} %copy-done.24) | copy-start | bytes 1572868
  401.6 26.2 %copy-start.35 = (bf16[128,1024]{1,0:T(8,128)(2,1)S(1)}, bf16[128,1024]{1,0:T(8,128)(2,1)}, u32[]{:S(2)}) copy-start(bf16[128,1024]{1,0:T(8,128)(2,1)} %copy-done.34) | copy-start | bytes 786436
  435.6 13.4 %collective-permute-start.2 = (bf16[2,1024,512]{2,1,0:T(8,128)(2,1)}, bf16[2,1024,512]{2,1,0:T(8,128)(2,1)S(1)}, u32[]{:S(2)}, u32[]{:S(2)}) collective-permute-start(bf16[2,1024,512]{2,1,0:T(8,128)(2,1)} %dynamic-slice_bitcast_fusion.1), channel_id=1, source_target_pairs={{0,1},{1,0},{2,3},{3,2},{4,5},{5,4},{6,7},{7,6},{8,9},{9,8},{10,11... | collective-permute-start | bytes 6291464 | tf_op jit(solution)/shard_map/ppermute | solution.py:78
  445.9 1.3 collective-permute-start.3
  453.9 134.3 %all-to-all-start.9 = ((bf16[64,40,512]{2,1,0:T(8,128)(2,1)}), bf16[64,40,512]{2,1,0:T(8,128)(2,1)S(1)}, u32[]{:S(2)}, u32[]{:S(2)}) async-start(bf16[64,40,512]{2,1,0:T(8,128)(2,1)} %pad_maximum_fusion), calls=%async_computation.11 | async-start | bytes 5242880 | tf_op jit(solution)/shard_map/all_to_all | solution.py:70
  588.3 16.6 %all-to-all-start.10 = ((bf16[4,784,128]{2,1,0:T(8,128)(2,1)}), bf16[4,784,128]{2,1,0:T(8,128)(2,1)}, u32[]{:S(2)}, u32[]{:S(2)}) async-start(bf16[4,784,128]{2,1,0:T(8,128)(2,1)} %pad_maximum_fusion.2), calls=%async_computation.14 | async-start | bytes 1605632 | tf_op jit(solution)/shard_map/all_to_all | solution.py:70
  (38 other events, 181.9 us)
Sparse Core Ops, SparseCore 0:
  35.7 76.9 all-gather.20
  115.0 44.3 all-gather.22
  161.1 17.0 all-gather.18
  179.7 23.8 all-gather.14
  205.1 14.6 all-gather.24
  221.4 26.4 all-gather.16
  249.6 31.4 all-gather.28
  282.7 13.5 all-gather.26
  312.5 45.1 reduce-scatter.4
  379.2 70.0 reduce-scatter.6
  453.1 99.4 reduce-scatter.8
  554.8 31.3 reduce-scatter.10
